TPU v7x, 32 devices: a whole 2x2x4 slice. The times are simulated.
32 devices in a mesh: sec: 2 (over y), row: 4 (over x, core), col: 4 (over z).
Axes of the slice: x: 2, y: 2, z: 4, core: 2. Of those that a mesh axis runs over, the one named last changes fastest.
Arguments:
- sketch: float32 [32, 64, 2048], P(None, ('sec', 'row'), 'col'), parts along dimension 1, may hold values from -6 to 6
- weights: float32 [8, 64, 2048], P(None, ('sec', 'row'), 'col'), parts along dimension 1, may hold values from 0.05 to 1
Outputs:
- basis: float32 [32, 64, 2048], P(None, ('sec', 'row'), 'col'), parts along dimension 1
- factor: float32 [64, 32], P('sec'), parts along dimension 0
There are 2 independent parts, one for each index of `sec`. A program takes and returns all parts, laid end to end along the dimension named above; each array names one. Nothing has to cross between parts.
All inputs are finite; a program needn't handle non-finite values.
Results may differ from a plain program's by a relative error of at most 0.0001.
Values sent between devices are 32-bit elements; how exact they have to be, the bound alone decides.
No kernel may reach another device: no remote copies, remote signals or barrier semaphores. Data moves between devices by JAX's collectives and lax.ppermute only.
A program may use at most 64 MiB of HBM per device.

v0:
```python
import functools

import jax
import jax.numpy as jnp
from jax import lax
from jax.experimental import pallas as pl
from jax.experimental.pallas import tpu as pltpu
from jax.sharding import PartitionSpec as P

NEIGHBOURS = ((-1, -1), (-1, 0), (-1, 1), (0, -1), (0, 1), (1, -1), (1, 0), (1, 1))
LANES = 128
PITCH = 8
HIGHEST = lax.Precision.HIGHEST


def call(kernel, out_shapes, *operands, scratch=()):
    return pl.pallas_call(
        kernel,
        out_shape=out_shapes,
        in_specs=[pl.BlockSpec(memory_space=pltpu.VMEM)] * len(operands),
        out_specs=[pl.BlockSpec(memory_space=pltpu.VMEM)] * len(out_shapes),
        scratch_shapes=scratch,
        compiler_params=pltpu.CompilerParams(vmem_limit_bytes=40 * 1024 * 1024),
    )(*operands)


def f32(*shape):
    return jax.ShapeDtypeStruct(shape, jnp.float32)


def sides_of(axis):
    place = lax.axis_index(axis)
    return place % 2 == 0, place > 0, place < lax.axis_size(axis) - 1


def pack_rows_kernel(joined, by_row, weights_by_row, *row_messages):
    rows, planes, _ = by_row.shape
    even_row, _, _ = sides_of("row")
    for row in range(rows):
        weights_by_row[row] = joined[planes:, row, :]
        by_row[row] = joined[:planes, row, :]
    for message, up in zip(row_messages, (even_row, jnp.logical_not(even_row))):
        start = jnp.where(up, rows - 2, 0)
        for slot in range(2):
            message[slot * planes : (slot + 1) * planes] = by_row[start + slot]
        message[2 * planes :] = weights_by_row[jnp.where(up, rows - 1, 0)]


def row_parts(by_row, weights_by_row, first_message, second_message, window):
    rows, planes, _ = by_row.shape
    even_row, has_below, has_above = sides_of("row")
    one, other = first_message[:, window], second_message[:, window]
    below = jnp.where(has_below, jnp.where(even_row, other, one), 0.0)
    above = jnp.where(has_above, jnp.where(even_row, one, other), 0.0)
    values = [below[:planes], below[planes : 2 * planes]]
    values += [by_row[row, :, window] for row in range(rows)]
    values += [above[:planes], above[planes : 2 * planes]]
    weights = [below[2 * planes :]]
    weights += [weights_by_row[row, :, window] for row in range(rows)]
    weights += [above[2 * planes :]]
    return values, weights


def strips_kernel(by_row, weights_by_row, first_message, second_message, left, right, *col_messages):
    planes, width = by_row.shape[1:]
    even_col, _, _ = sides_of("col")
    lane = lax.broadcasted_iota(jnp.int32, (1, LANES), 1)
    own = PITCH - 2
    for target, start, low, at in ((left, 0, 2, 0), (right, width - LANES, 0, LANES - own)):
        values, weights = row_parts(by_row, weights_by_row, first_message, second_message, pl.ds(start, LANES))
        for part, some, skip in ((slice(None, planes), values, 0), (slice(planes, None), weights, 1)):
            total = None
            for row, value in enumerate(some):
                place = PITCH * (row + skip) + low
                moved = pltpu.roll(value, (place - at) % LANES, 1)
                moved = jnp.where((lane >= place) & (lane < place + own), moved, 0.0)
                total = moved if total is None else total + moved
            target[part] = total
    to_left, to_right = folded(left[...], 2), folded(right[...], own - 2)
    for message, up in zip(col_messages, (even_col, jnp.logical_not(even_col))):
        message[...] = jnp.where(up, to_right, to_left)


def folded(strip, spot):
    lane = lax.broadcasted_iota(jnp.int32, (1, LANES), 1)
    groups = strip.shape[0] // 8
    pieces = []
    for group in range(groups):
        target = 2 * group if group < groups - 1 else 0
        moved = rolled(strip[8 * group : 8 * (group + 1)], target - spot)
        pieces.append(jnp.where((lane % PITCH) // 2 == target // 2, moved, 0.0))
    return jnp.concatenate([functools.reduce(jnp.add, pieces[:-1]), pieces[-1]], axis=0)


def unfolded(message, spot, planes):
    lane = lax.broadcasted_iota(jnp.int32, (1, LANES), 1)
    pieces = [rolled(message[:8], spot - 2 * group) for group in range(planes // 8)] + [rolled(message[8:], spot)]
    return jnp.where((lane % PITCH) // 2 == spot // 2, jnp.concatenate(pieces, axis=0), 0.0)


def rolled(value, shift):
    return pltpu.roll(value, shift % LANES, 1) if shift % LANES else value


def apply_operator(rows3, weight_rows):
    width = rows3[1].shape[1]
    degree = jnp.sum(weight_rows, axis=0, keepdims=True)
    total = degree * rows3[1]
    sides = {-1: None, 1: None}
    for position, (up, across) in enumerate(NEIGHBOURS):
        weight = weight_rows[position : position + 1]
        value = rows3[up + 1]
        if across == 0:
            total = total + weight * value
        else:
            shifted = pltpu.roll(weight_rows, across % width, 1)[position : position + 1]
            term = shifted * value
            sides[across] = term if sides[across] is None else sides[across] + term
    for across, value in sides.items():
        total = total + pltpu.roll(value, (-across) % width, 1)
    return total


def gram_of(value, other):
    return lax.dot_general(
        value, other, (((1,), (1,)), ((), ())), precision=HIGHEST, preferred_element_type=jnp.float32
    )


def split(value):
    high = value.astype(jnp.bfloat16)
    rest = value - high.astype(jnp.float32)
    middle = rest.astype(jnp.bfloat16)
    low = (rest - middle.astype(jnp.float32)).astype(jnp.bfloat16)
    return high, middle, low


def early_kernel(by_row, weights_by_row, first_message, second_message, second, grams, middle):
    rows, planes, width = by_row.shape
    values, weights = row_parts(by_row, weights_by_row, first_message, second_message, slice(None))
    col = lax.broadcasted_iota(jnp.int32, (1, width), 1)
    inner = (col >= 2) & (col < width - 2)
    for row in range(rows + 2):
        middle[row] = apply_operator(values[row : row + 3], weights[row])
    gram = [jnp.zeros((planes, planes), jnp.float32)] * 2
    for row in range(rows):
        image = apply_operator([middle[row], middle[row + 1], middle[row + 2]], weights[row + 1])
        for at, part in enumerate(split(image)):
            second[row, at * planes : (at + 1) * planes] = part
        for at, value in enumerate((middle[row + 1], image)):
            gram[at] = gram[at] + gram_of(jnp.where(inner, value, 0.0), value)
    grams[:, :planes] = gram[0]
    grams[:, planes:] = gram[1]


def apply_on_strip(values, weights):
    total = jnp.sum(weights, axis=0, keepdims=True) * values
    for position, (up, across) in enumerate(NEIGHBOURS):
        moved = pltpu.roll(values, (-PITCH * up - across) % LANES, 1)
        total = total + weights[position : position + 1] * moved
    return total


def late_kernel(rows, left, right, first_message, second_message, early_grams, grams, edges):
    planes = early_grams.shape[0]
    even_col, has_left, has_right = sides_of("col")
    one, other = first_message[...], second_message[...]
    lane = lax.broadcasted_iota(jnp.int32, (1, LANES), 1)
    spot, row = lane % PITCH, lane // PITCH
    gram = [early_grams[:, :planes], early_grams[:, planes:]]
    for side, (strip, present, halo) in enumerate(
        ((left, has_left, jnp.where(even_col, other, one)), (right, has_right, jnp.where(even_col, one, other)))
    ):
        whole = strip[...] + jnp.where(present, unfolded(halo, side * (PITCH - 2), planes), 0.0)
        values, weights = whole[:planes], whole[planes:]
        low = 2 if side == 0 else PITCH - 4
        outer = (spot >= low) & (spot < low + 2) & (row >= 2) & (row < rows + 2)
        for at in range(2):
            values = apply_on_strip(values, weights)
            gram[at] = gram[at] + gram_of(jnp.where(outer, values, 0.0), values)
        edges[:, side * LANES : (side + 1) * LANES] = values
    at_row = lax.broadcasted_iota(jnp.int32, (planes, planes), 0)
    at_col = lax.broadcasted_iota(jnp.int32, (planes, planes), 1)
    mixed = jnp.where(at_row >= at_col, gram[0], gram[1])
    diagonal = jnp.sum(jnp.where(at_row == at_col, gram[1], 0.0), axis=0, keepdims=True)
    block = jnp.concatenate([mixed[8 * g : 8 * (g + 1)] for g in range(planes // 8)], axis=1)
    last = jnp.concatenate([diagonal] * (LANES // planes), axis=1)
    for target in range(grams.shape[0]):
        for at in range(8):
            grams[target, :, at * LANES : (at + 1) * LANES] = block[at : at + 1]
        grams[target, :, 8 * LANES :] = last


def eliminate(grams, planes):
    lane = lax.broadcasted_iota(jnp.int32, (8, LANES), 1)
    sub = lax.broadcasted_iota(jnp.int32, (8, LANES), 0)
    first_half = lane < 2 * planes
    groups = planes // 8
    sources = [[gram[8 * g : 8 * (g + 1)] for g in range(groups)] for gram in grams]
    state = []
    for g in range(groups):
        unit = jnp.where(sub + 8 * g == lane % (2 * planes) - planes, 1.0, 0.0)
        unit = unit[:, planes : 2 * planes]
        state.append(jnp.concatenate([sources[0][g], unit, sources[1][g], unit], axis=1))
    columns = []
    for j in range(planes):
        columns.append(
            {
                g: jnp.where(
                    first_half,
                    jnp.broadcast_to(sources[0][g][:, j : j + 1], (8, LANES)),
                    jnp.broadcast_to(sources[1][g][:, j : j + 1], (8, LANES)),
                )
                for g in range(j // 8, groups)
            }
        )
    scale = [jnp.ones((8, LANES), jnp.float32)] * groups
    for step in range(planes):
        own, at = step // 8, step % 8
        column = columns[step]
        root = lax.rsqrt(jnp.broadcast_to(column[own][at : at + 1], (8, LANES)))
        inverse = root * root
        scale[own] = jnp.where(sub == at, root, scale[own])
        factors = {g: value * inverse for g, value in column.items()}
        factors[own] = jnp.where(sub > at, factors[own], 0.0)
        for j in range(step + 1, planes):
            entry = jnp.broadcast_to(column[j // 8][j % 8 : j % 8 + 1], (8, LANES))
            for g in columns[j]:
                columns[j][g] = columns[j][g] - factors[g] * entry
        pivot_row = jnp.broadcast_to(state[own][at : at + 1], (8, LANES))
        for g in range(own, groups):
            state[g] = state[g] - factors[g] * pivot_row
    return jnp.concatenate([state[g] * scale[g] for g in range(groups)], axis=0)


def finish_kernel(pixel_count, second, edges, parts, basis, factor):
    planes = factor.shape[0]
    rows, _, width = second.shape
    at_row = lax.broadcasted_iota(jnp.int32, (planes, planes), 0)
    at_col = lax.broadcasted_iota(jnp.int32, (planes, planes), 1)
    block = tree_sum([parts[at] for at in range(parts.shape[0])]) / pixel_count
    block = [block[:, at * LANES : (at + 1) * LANES] for at in range(9)]
    mixed, diagonal = jnp.concatenate(block[:8], axis=0), block[8][:, :planes]
    mixed = jnp.concatenate([mixed[:, at * planes : (at + 1) * planes] for at in range(LANES // planes)], axis=0)
    flipped = mixed.T
    first = jnp.where(at_row >= at_col, mixed, flipped)
    second_gram = jnp.where(at_row < at_col, mixed, jnp.where(at_row > at_col, flipped, diagonal))
    state = eliminate([first, second_gram], planes)
    first_inverse = state[:, planes : 2 * planes]
    product_upper = jnp.where(at_col >= at_row, state[:, 2 * planes : 3 * planes], 0.0)
    product_inverse = jnp.where(at_col <= at_row, state[:, 3 * planes :], 0.0)
    factor[...] = jnp.where(at_col >= at_row, gram_of(product_upper, first_inverse), 0.0)
    high, middle, low = split(product_inverse)
    left_side = jnp.concatenate([high, high, middle, high, low, middle], axis=1)

    def solved(high, middle, low):
        right_side = jnp.concatenate([high, middle, high, low, high, middle], axis=0)
        return jnp.dot(left_side, right_side, preferred_element_type=jnp.float32)

    lane = lax.broadcasted_iota(jnp.int32, (1, LANES), 1)
    outer = solved(*split(edges[...]))
    for row in range(rows):
        value = solved(*(second[row, at * planes : (at + 1) * planes] for at in range(3)))
        place = PITCH * (row + 2)
        low_end = pltpu.roll(outer[:, :LANES], LANES - (place + 2), 1)
        high_end = pltpu.roll(outer[:, LANES:], (LANES - 2 - (place + PITCH - 4)) % LANES, 1)
        basis[:, row, :LANES] = jnp.where(lane < 2, low_end, value[:, :LANES])
        basis[:, row, LANES : width - LANES] = value[:, LANES : width - LANES]
        basis[:, row, width - LANES :] = jnp.where(lane >= LANES - 2, high_end, value[:, width - LANES :])


def tree_sum(parts):
    while len(parts) > 1:
        parts = [sum(parts[at + 1 : at + 2], parts[at]) for at in range(0, len(parts), 2)]
    return parts[0]


def swap(value, axis, pairing):
    rows, cols = lax.axis_size("row"), lax.axis_size("col")
    pairs = []
    for row in range(rows):
        for col in range(cols):
            place, count = (row, rows) if axis == "row" else (col, cols)
            other = place + 1 if place % 2 == pairing else place - 1
            if not 0 <= other < count:
                partner = (row, col ^ 1) if axis == "row" else (row ^ 1, col)
            else:
                partner = (other, col) if axis == "row" else (row, other)
            pairs.append((row * cols + col, partner[0] * cols + partner[1]))
    return lax.ppermute(value, ("row", "col"), pairs)


def on_device(sketch, weights):
    planes, rows, width = sketch.shape
    group = lax.axis_size("row") * lax.axis_size("col")
    by_row, weights_by_row, *messages = call(
        pack_rows_kernel,
        [f32(rows, planes, width), f32(rows, 8, width)] + [f32(2 * planes + 8, width)] * 2,
        jnp.concatenate([sketch, weights], axis=0),
    )
    from_rows = [swap(messages[pairing], "row", pairing) for pairing in (1, 0)][::-1]
    left, right, *messages = call(strips_kernel, [f32(planes + 8, LANES)] * 2 + [f32(16, LANES)] * 2, by_row, weights_by_row, *from_rows)
    from_cols = [swap(message, "col", pairing) for pairing, message in enumerate(messages)]
    second, early_grams = call(
        early_kernel,
        [jax.ShapeDtypeStruct((rows, 3 * planes, width), jnp.bfloat16), f32(planes, 2 * planes)],
        by_row,
        weights_by_row,
        *from_rows,
        scratch=[pltpu.VMEM((rows + 2, planes, width), jnp.float32)],
    )
    grams, edges = call(
        functools.partial(late_kernel, rows),
        [f32(group, 1, 9 * LANES), f32(planes, 2 * LANES)],
        left,
        right,
        *from_cols,
        early_grams,
    )
    parts = lax.all_to_all(grams, ("row", "col"), 0, 0, tiled=True)
    return call(
        functools.partial(finish_kernel, float(rows * width * group)),
        [f32(planes, rows, width), f32(planes, planes)],
        second,
        edges,
        parts,
    )


def solution(mesh):
    return jax.shard_map(
        on_device,
        mesh=mesh,
        in_specs=(P(None, ("sec", "row"), "col"), P(None, ("sec", "row"), "col")),
        out_specs=(P(None, ("sec", "row"), "col"), P("sec", None)),
        check_vma=False,
    )
```

profile of v0, /device:TPU:0, one launch (start us, length us, event | category | flops | bytes accessed | tf_op | source)
XLA Modules:
  0.0 28.1 jit_solution(7096613724967181033)
XLA Ops:
  0.6 1.2 %pad_maximum_fusion.joined = f32[40,8,512]{2,1,0:T(8,128)S(1)} fusion(f32[8,8,512]{2,1,0:T(8,128)} %param.3, f32[32,8,512]{2,1,0:T(8,128)} %param.2), kind=kLoop, calls=%fused_computation | loop fusion | flops 163840 | bytes 1310720 | tf_op jit(solution)/shard_map/concatenate | solution.py:299
  1.8 0.2 shard_map.41
  2.0 0.5 %collective-permute-start = (f32[72,512]{1,0:T(8,128)S(1)}, f32[72,512]{1,0:T(8,128)S(1)}, u32[]{:S(2)}, u32[]{:S(2)}) collective-permute-start(f32[72,512]{1,0:T(8,128)S(1)} %get-tuple-element.16), channel_id=1, source_target_pairs={{0,4},{1,5},{2,6},{3,7},{4,0},{5,1},{6,2},{7,3},{8,12},{9,13},{10,... | collective-permute-start | bytes 442376 | tf_op jit(solution)/shard_map/ppermute | solution.py:290
  2.5 2.6 %collective-permute-start.1 = (f32[72,512]{1,0:T(8,128)S(1)}, f32[72,512]{1,0:T(8,128)S(1)}, u32[]{:S(2)}, u32[]{:S(2)}) collective-permute-start(f32[72,512]{1,0:T(8,128)S(1)} %get-tuple-element.17), channel_id=1, source_target_pairs={{0,1},{1,0},{2,3},{3,2},{4,8},{5,9},{6,10},{7,11},{8,4},{9,5},{10,... | collective-permute-start | bytes 442376 | tf_op jit(solution)/shard_map/ppermute | solution.py:290
  5.1 0.0 collective-permute-done.first_message
  5.1 3.1 %collective-permute-done.1.second_message = f32[72,512]{1,0:T(8,128)S(1)} collective-permute-done((f32[72,512]{1,0:T(8,128)S(1)}, f32[72,512]{1,0:T(8,128)S(1)}, u32[]{:S(2)}, u32[]{:S(2)}) %collective-permute-start.1) | collective-permute-done | bytes 147488 | tf_op jit(solution)/shard_map/ppermute | solution.py:290
  8.2 0.2 shard_map.43
  8.5 2.1 %collective-permute-start.2 = (f32[16,128]{1,0:T(8,128)S(1)}, f32[16,128]{1,0:T(8,128)S(1)}, u32[]{:S(2)}, u32[]{:S(2)}) collective-permute-start(f32[16,128]{1,0:T(8,128)S(1)} %get-tuple-element.21), channel_id=1, source_target_pairs={{0,1},{1,0},{2,3},{3,2},{4,5},{5,4},{6,7},{7,6},{8,9},{9,8},{10,11... | collective-permute-start | bytes 24584 | tf_op jit(solution)/shard_map/ppermute | solution.py:290
  10.6 0.0 collective-permute-start.3
  10.6 2.1 %shard_map.42 = (bf16[8,96,512]{2,1,0:T(8,128)(2,1)S(1)}, f32[32,64]{1,0:T(8,128)S(1)}) custom-call(f32[8,32,512]{2,1,0:T(8,128)S(1)} %get-tuple-element.14.by_row, f32[8,8,512]{2,1,0:T(8,128)S(1)} %get-tuple-element.15.weights_by_row, f32[72,512]{1,0:T(8,128)S(1)} %collective-permute-done.first_message, f32[72,512]{1,0:T(8,128)S(1)} %collective-permute-done.1.second_message), custom_call_target="tpu_custom_call" | custom-call | tf_op jit(solution)/shard_map/pallas_call | solution.py:17
  12.7 0.0 collective-permute-done.2.first_message
  12.7 0.0 collective-permute-done.3.second_message
  12.7 0.8 %shard_map.44 = (f32[16,1,1152]{2,1,0:T(1,128)S(1)}, f32[32,256]{1,0:T(8,128)S(1)}) custom-call(f32[40,128]{1,0:T(8,128)S(1)} %get-tuple-element.19.left, f32[40,128]{1,0:T(8,128)S(1)} %get-tuple-element.20.right, f32[16,128]{1,0:T(8,128)S(1)} %collective-permute-done.2.first_message, f32[16,128]{1,0:T(8,128)S(1)} %collective-permute-done.3.second_message, ...), custom_call_target="tpu_custom_call" | custom-call | tf_op jit(solution)/shard_map/pallas_call | solution.py:17
  13.5 12.4 %all_to_all.5.parts = f32[16,1,1152]{2,1,0:T(1,128)S(1)} all-to-all(f32[16,1,1152]{2,1,0:T(1,128)S(1)} %get-tuple-element.25), channel_id=1, replica_groups=mesh['sec'=2,'row'=4,'col'=4] {'row','col'}, dimensions={0} | all-to-all | bytes 147456 | tf_op jit(solution)/shard_map/all_to_all | solution.py:320
  25.9 2.2 %shard_map.45 = (f32[32,8,512]{2,1,0:T(8,128)}, f32[32,32]{1,0:T(8,128)}) custom-call(bf16[8,96,512]{2,1,0:T(8,128)(2,1)S(1)} %get-tuple-element.18.second, f32[32,256]{1,0:T(8,128)S(1)} %get-tuple-element.24.edges, f32[16,1,1152]{2,1,0:T(1,128)S(1)} %all_to_all.5.parts), custom_call_target="tpu_custom_call" | custom-call | tf_op jit(solution)/shard_map/pallas_call | solution.py:17
Async XLA Ops:
  2.0 3.2 %collective-permute-start = (f32[72,512]{1,0:T(8,128)S(1)}, f32[72,512]{1,0:T(8,128)S(1)}, u32[]{:S(2)}, u32[]{:S(2)}) collective-permute-start(f32[72,512]{1,0:T(8,128)S(1)} %get-tuple-element.16), channel_id=1, source_target_pairs={{0,4},{1,5},{2,6},{3,7},{4,0},{5,1},{6,2},{7,3},{8,12},{9,13},{10,... | collective-permute-start | bytes 442376 | tf_op jit(solution)/shard_map/ppermute | solution.py:290
  2.5 5.8 %collective-permute-start.1 = (f32[72,512]{1,0:T(8,128)S(1)}, f32[72,512]{1,0:T(8,128)S(1)}, u32[]{:S(2)}, u32[]{:S(2)}) collective-permute-start(f32[72,512]{1,0:T(8,128)S(1)} %get-tuple-element.17), channel_id=1, source_target_pairs={{0,1},{1,0},{2,3},{3,2},{4,8},{5,9},{6,10},{7,11},{8,4},{9,5},{10,... | collective-permute-start | bytes 442376 | tf_op jit(solution)/shard_map/ppermute | solution.py:290
  8.5 4.2 %collective-permute-start.2 = (f32[16,128]{1,0:T(8,128)S(1)}, f32[16,128]{1,0:T(8,128)S(1)}, u32[]{:S(2)}, u32[]{:S(2)}) collective-permute-start(f32[16,128]{1,0:T(8,128)S(1)} %get-tuple-element.21), channel_id=1, source_target_pairs={{0,1},{1,0},{2,3},{3,2},{4,5},{5,4},{6,7},{7,6},{8,9},{9,8},{10,11... | collective-permute-start | bytes 24584 | tf_op jit(solution)/shard_map/ppermute | solution.py:290
  10.6 2.1 %collective-permute-start.3 = (f32[16,128]{1,0:T(8,128)S(1)}, f32[16,128]{1,0:T(8,128)S(1)}, u32[]{:S(2)}, u32[]{:S(2)}) collective-permute-start(f32[16,128]{1,0:T(8,128)S(1)} %get-tuple-element.22), channel_id=1, source_target_pairs={{0,4},{1,2},{2,1},{3,7},{4,0},{5,6},{6,5},{7,3},{8,12},{9,10},{10,... | collective-permute-start | bytes 24584 | tf_op jit(solution)/shard_map/ppermute | solution.py:290
where the time goes:
time: 28.3 us; the launch traced here: 28.1 us
  blocking collectives  12.4 us (44%)
  Pallas kernels  5.5 us (19%)
  starting transfers between devices  5.25 us (19%)
  waiting for transfers between devices  3.13 us (11%)
  other arithmetic  1.16 us (4%)
  between operations  0.66 us (2%)
    all_to_all x1, blocking collectives, on_device(): parts = lax.all_to_all(grams, ('row', 'col'), 0, 0, tiled=True)  12.4 us
    pallas_call x5, Pallas kernels, call(): pl.pallas_call(kernel, out_shape=out_shapes, in_specs=[pl.BlockSpec(memor...  5.5 us
    ppermute x4, starting transfers between devices, swap(): return lax.ppermute(value, ('row', 'col'), pairs)  5.25 us
    ppermute x4, waiting for transfers between devices, swap(): return lax.ppermute(value, ('row', 'col'), pairs)  3.13 us
    concatenate x1, other arithmetic, on_device(): jnp.concatenate([sketch, weights], axis=0)  1.16 us
  transfers between devices with their start and end apart: 4, of which 1 were waited for; matrix products, arithmetic and copies ran while one was open for 0% of the time, Pallas kernels for 7%

commit v1 on v0

--- a/solution.py
+++ b/solution.py
@@ -1,4 +1,5 @@
 import functools
+import itertools
 
 import jax
 import jax.numpy as jnp
@@ -13,13 +14,14 @@
 HIGHEST = lax.Precision.HIGHEST
 
 
-def call(kernel, out_shapes, *operands, scratch=()):
+def call(kernel, out_shapes, *operands, scratch=(), cost=None):
     return pl.pallas_call(
         kernel,
         out_shape=out_shapes,
         in_specs=[pl.BlockSpec(memory_space=pltpu.VMEM)] * len(operands),
         out_specs=[pl.BlockSpec(memory_space=pltpu.VMEM)] * len(out_shapes),
         scratch_shapes=scratch,
+        cost_estimate=cost,
         compiler_params=pltpu.CompilerParams(vmem_limit_bytes=40 * 1024 * 1024),
     )(*operands)
 
@@ -30,54 +32,82 @@
 
 def sides_of(axis):
     place = lax.axis_index(axis)
-    return place % 2 == 0, place > 0, place < lax.axis_size(axis) - 1
-
-
-def pack_rows_kernel(joined, by_row, weights_by_row, *row_messages):
-    rows, planes, _ = by_row.shape
-    even_row, _, _ = sides_of("row")
+    return place % 2 == 1, place > 0, place < lax.axis_size(axis) - 1
+
+
+def pack_rows_kernel(joined, by_row, weights_by_row, left, right, *messages):
+    corner_messages, bulk_messages = messages[:2], messages[2:]
+    rows, planes, width = by_row.shape
+    odd_row, _, _ = sides_of("row")
+    lane = lax.broadcasted_iota(jnp.int32, (1, LANES), 1)
+    own = PITCH - 2
+    for target, start, low, at in ((left, 0, 2, 0), (right, width - LANES, 0, LANES - own)):
+        total = None
+        for row in range(rows):
+            place = PITCH * (row + 2) + low
+            moved = rolled(joined[:, row, start : start + LANES], place - at)
+            moved = jnp.where((lane >= place) & (lane < place + own), moved, 0.0)
+            total = moved if total is None else total + moved
+        target[...] = total
+    pair = 2 * PITCH
+    for message, up in zip(corner_messages, (odd_row, jnp.logical_not(odd_row))):
+        pieces = []
+        for group in range(planes // 8 + 1):
+            piece = None
+            for side, strip in enumerate((left, right)):
+                target = (2 * group + side) * pair if group < planes // 8 else side * pair
+                value = strip[8 * group : 8 * (group + 1)]
+                moved = jnp.where(up, rolled(value, target - PITCH * rows), rolled(value, target - 2 * PITCH))
+                moved = jnp.where(lane // pair == target // pair, moved, 0.0)
+                piece = moved if piece is None else piece + moved
+            pieces.append(piece)
+        message[:8] = functools.reduce(jnp.add, pieces[:-1])
+        message[8:] = pieces[-1]
     for row in range(rows):
         weights_by_row[row] = joined[planes:, row, :]
         by_row[row] = joined[:planes, row, :]
-    for message, up in zip(row_messages, (even_row, jnp.logical_not(even_row))):
+    for message, up in zip(bulk_messages, (odd_row, jnp.logical_not(odd_row))):
         start = jnp.where(up, rows - 2, 0)
         for slot in range(2):
             message[slot * planes : (slot + 1) * planes] = by_row[start + slot]
         message[2 * planes :] = weights_by_row[jnp.where(up, rows - 1, 0)]
 
 
-def row_parts(by_row, weights_by_row, first_message, second_message, window):
+def row_parts(by_row, weights_by_row, first_message, second_message):
     rows, planes, _ = by_row.shape
-    even_row, has_below, has_above = sides_of("row")
-    one, other = first_message[:, window], second_message[:, window]
-    below = jnp.where(has_below, jnp.where(even_row, other, one), 0.0)
-    above = jnp.where(has_above, jnp.where(even_row, one, other), 0.0)
+    odd_row, has_below, has_above = sides_of("row")
+    one, other = first_message[...], second_message[...]
+    below = jnp.where(has_below, jnp.where(odd_row, other, one), 0.0)
+    above = jnp.where(has_above, jnp.where(odd_row, one, other), 0.0)
     values = [below[:planes], below[planes : 2 * planes]]
-    values += [by_row[row, :, window] for row in range(rows)]
+    values += [by_row[row] for row in range(rows)]
     values += [above[:planes], above[planes : 2 * planes]]
     weights = [below[2 * planes :]]
-    weights += [weights_by_row[row, :, window] for row in range(rows)]
+    weights += [weights_by_row[row] for row in range(rows)]
     weights += [above[2 * planes :]]
     return values, weights
 
 
-def strips_kernel(by_row, weights_by_row, first_message, second_message, left, right, *col_messages):
-    planes, width = by_row.shape[1:]
-    even_col, _, _ = sides_of("col")
-    lane = lax.broadcasted_iota(jnp.int32, (1, LANES), 1)
-    own = PITCH - 2
-    for target, start, low, at in ((left, 0, 2, 0), (right, width - LANES, 0, LANES - own)):
-        values, weights = row_parts(by_row, weights_by_row, first_message, second_message, pl.ds(start, LANES))
-        for part, some, skip in ((slice(None, planes), values, 0), (slice(planes, None), weights, 1)):
-            total = None
-            for row, value in enumerate(some):
-                place = PITCH * (row + skip) + low
-                moved = pltpu.roll(value, (place - at) % LANES, 1)
-                moved = jnp.where((lane >= place) & (lane < place + own), moved, 0.0)
-                total = moved if total is None else total + moved
-            target[part] = total
-    to_left, to_right = folded(left[...], 2), folded(right[...], own - 2)
-    for message, up in zip(col_messages, (even_col, jnp.logical_not(even_col))):
+def strips_kernel(rows, own_left, own_right, first_message, second_message, left, right, *col_messages):
+    planes = own_left.shape[0] - 8
+    odd_row, has_below, has_above = sides_of("row")
+    odd_col, _, _ = sides_of("col")
+    one, other = first_message[...], second_message[...]
+    lane = lax.broadcasted_iota(jnp.int32, (1, LANES), 1)
+    pair = 2 * PITCH
+    halos = (
+        (jnp.where(has_below, jnp.where(odd_row, other, one), 0.0), 0),
+        (jnp.where(has_above, jnp.where(odd_row, one, other), 0.0), PITCH * (rows + 2)),
+    )
+    for side, (strip, target) in enumerate(((own_left, left), (own_right, right))):
+        total = strip[...]
+        for halo, place in halos:
+            pieces = [rolled(halo[:8], place - (2 * group + side) * pair) for group in range(planes // 8)]
+            pieces.append(rolled(halo[8:], place - side * pair))
+            total = total + jnp.where(lane // pair == place // pair, jnp.concatenate(pieces, axis=0), 0.0)
+        target[...] = total
+    to_left, to_right = folded(left[...], 2), folded(right[...], PITCH - 4)
+    for message, up in zip(col_messages, (odd_col, jnp.logical_not(odd_col))):
         message[...] = jnp.where(up, to_right, to_left)
 
 
@@ -137,7 +167,7 @@
 
 def early_kernel(by_row, weights_by_row, first_message, second_message, second, grams, middle):
     rows, planes, width = by_row.shape
-    values, weights = row_parts(by_row, weights_by_row, first_message, second_message, slice(None))
+    values, weights = row_parts(by_row, weights_by_row, first_message, second_message)
     col = lax.broadcasted_iota(jnp.int32, (1, width), 1)
     inner = (col >= 2) & (col < width - 2)
     for row in range(rows + 2):
@@ -163,13 +193,13 @@
 
 def late_kernel(rows, left, right, first_message, second_message, early_grams, grams, edges):
     planes = early_grams.shape[0]
-    even_col, has_left, has_right = sides_of("col")
+    odd_col, has_left, has_right = sides_of("col")
     one, other = first_message[...], second_message[...]
     lane = lax.broadcasted_iota(jnp.int32, (1, LANES), 1)
     spot, row = lane % PITCH, lane // PITCH
     gram = [early_grams[:, :planes], early_grams[:, planes:]]
     for side, (strip, present, halo) in enumerate(
-        ((left, has_left, jnp.where(even_col, other, one)), (right, has_right, jnp.where(even_col, one, other)))
+        ((left, has_left, jnp.where(odd_col, other, one)), (right, has_right, jnp.where(odd_col, one, other)))
     ):
         whole = strip[...] + jnp.where(present, unfolded(halo, side * (PITCH - 2), planes), 0.0)
         values, weights = whole[:planes], whole[planes:]
@@ -276,30 +306,40 @@
 
 
 def swap(value, axis, pairing):
-    rows, cols = lax.axis_size("row"), lax.axis_size("col")
+    names = ("sec", "row", "col")
+    shape = [lax.axis_size(name) for name in names]
+    at = names.index(axis)
+
+    def number(place):
+        return (place[0] * shape[1] + place[1]) * shape[2] + place[2]
+
     pairs = []
-    for row in range(rows):
-        for col in range(cols):
-            place, count = (row, rows) if axis == "row" else (col, cols)
-            other = place + 1 if place % 2 == pairing else place - 1
-            if not 0 <= other < count:
-                partner = (row, col ^ 1) if axis == "row" else (row ^ 1, col)
-            else:
-                partner = (other, col) if axis == "row" else (row, other)
-            pairs.append((row * cols + col, partner[0] * cols + partner[1]))
-    return lax.ppermute(value, ("row", "col"), pairs)
+    for place in itertools.product(*(range(extent) for extent in shape)):
+        partner = list(place)
+        partner[at] += 1 if place[at] % 2 != pairing else -1
+        if not 0 <= partner[at] < shape[at]:
+            partner[at] = place[at]
+            partner[at - 1] ^= 1
+        pairs.append((number(place), number(partner)))
+    return lax.ppermute(value, names, pairs)
 
 
 def on_device(sketch, weights):
     planes, rows, width = sketch.shape
     group = lax.axis_size("row") * lax.axis_size("col")
-    by_row, weights_by_row, *messages = call(
+    side = f32(planes + 8, LANES)
+    by_row, weights_by_row, left, right, *messages = call(
         pack_rows_kernel,
-        [f32(rows, planes, width), f32(rows, 8, width)] + [f32(2 * planes + 8, width)] * 2,
+        [f32(rows, planes, width), f32(rows, 8, width), side, side]
+        + [f32(16, LANES)] * 2
+        + [f32(2 * planes + 8, width)] * 2,
         jnp.concatenate([sketch, weights], axis=0),
     )
-    from_rows = [swap(messages[pairing], "row", pairing) for pairing in (1, 0)][::-1]
-    left, right, *messages = call(strips_kernel, [f32(planes + 8, LANES)] * 2 + [f32(16, LANES)] * 2, by_row, weights_by_row, *from_rows)
+    corners = [swap(message, "row", pairing) for pairing, message in enumerate(messages[:2])]
+    from_rows = [swap(message, "row", pairing) for pairing, message in enumerate(messages[2:])]
+    left, right, *messages = call(
+        functools.partial(strips_kernel, rows), [side, side] + [f32(16, LANES)] * 2, left, right, *corners, cost=pl.CostEstimate(flops=2000000000, bytes_accessed=4000000, transcendentals=0)
+    )
     from_cols = [swap(message, "col", pairing) for pairing, message in enumerate(messages)]
     second, early_grams = call(
         early_kernel,

time: 28.3 us -> 27.2 us (0.961)
  starting transfers between devices: 5.25 us -> 8.36 us
  waiting for transfers between devices: 3.13 us -> 0.04 us
  blocking collectives: 12.4 us -> 11.2 us
    ppermute x4 -> x6, starting transfers between devices: 5.25 us -> 8.36 us  [swap(): return lax.ppermute(value, names, pairs)]
    ppermute x4 -> x6, waiting for transfers between devices: 3.13 us -> 0.04 us  [swap(): return lax.ppermute(value, names, pairs)]
    all_to_all x1, blocking collectives: 12.4 us -> 11.2 us  [on_device(): parts = lax.all_to_all(grams, ('row', 'col'), 0, 0, tiled=True)]
  transfers between devices with their start and end apart: 4 -> 6, of which waited for: 1 -> 0; matrix products, arithmetic and copies ran while one was open for 0% -> 0% of each run, Pallas kernels for 7% -> 8%
where the time goes in v1:
time: 27.2 us; the launch traced here: 27 us
  blocking collectives  11.2 us (41%)
  starting transfers between devices  8.36 us (31%)
  Pallas kernels  5.59 us (21%)
  other arithmetic  1.16 us (4%)
  between operations  0.66 us (2%)
    all_to_all x1, blocking collectives, on_device(): parts = lax.all_to_all(grams, ('row', 'col'), 0, 0, tiled=True)  11.2 us
    ppermute x6, starting transfers between devices, swap(): return lax.ppermute(value, names, pairs)  8.36 us
    pallas_call x5, Pallas kernels, call(): pl.pallas_call(kernel, out_shape=out_shapes, in_specs=[pl.BlockSpec(memor...  5.59 us
    concatenate x1, other arithmetic, on_device(): jnp.concatenate([sketch, weights], axis=0)  1.16 us
  transfers between devices with their start and end apart: 6, of which 0 were waited for; matrix products, arithmetic and copies ran while one was open for 0% of the time, Pallas kernels for 8%

profile of v1, /device:TPU:0, one launch (start us, length us, event | category | flops | bytes accessed | tf_op | source)
XLA Modules:
  0.0 27.0 jit_solution(18244351554972675485)
XLA Ops:
  0.6 1.2 %pad_maximum_fusion.joined = f32[40,8,512]{2,1,0:T(8,128)S(1)} fusion(f32[8,8,512]{2,1,0:T(8,128)} %param.3, f32[32,8,512]{2,1,0:T(8,128)} %param.2), kind=kLoop, calls=%fused_computation | loop fusion | flops 163840 | bytes 1310720 | tf_op jit(solution)/shard_map/concatenate | solution.py:336
  1.8 0.3 %shard_map.41 = (f32[8,32,512]{2,1,0:T(8,128)S(1)}, f32[8,8,512]{2,1,0:T(8,128)S(1)}, f32[40,128]{1,0:T(8,128)S(1)}, f32[40,128]{1,0:T(8,128)S(1)}, f32[16,128]{...) custom-call(f32[40,8,512]{2,1,0:T(8,128)S(1)} %pad_maximum_fusion.joined), custom_call_target="tpu_custom_call" | custom-call | tf_op jit(solution)/shard_map/pallas_call | solution.py:18
  2.1 3.0 %collective-permute-start.2 = (f32[16,128]{1,0:T(8,128)S(1)}, f32[16,128]{1,0:T(8,128)S(1)}, u32[]{:S(2)}, u32[]{:S(2)}) collective-permute-start(f32[16,128]{1,0:T(8,128)S(1)} %get-tuple-element.25), channel_id=1, source_target_pairs={{0,16},{1,17},{2,18},{3,19},{4,8},{5,9},{6,10},{7,11},{8,4},{9,5},... | collective-permute-start | bytes 24584 | tf_op jit(solution)/shard_map/ppermute | solution.py:324
  5.2 0.1 collective-permute-start.3
  5.2 1.5 %collective-permute-start = (f32[72,512]{1,0:T(8,128)S(1)}, f32[72,512]{1,0:T(8,128)S(1)}, u32[]{:S(2)}, u32[]{:S(2)}) collective-permute-start(f32[72,512]{1,0:T(8,128)S(1)} %get-tuple-element.20), channel_id=1, source_target_pairs={{0,16},{1,17},{2,18},{3,19},{4,8},{5,9},{6,10},{7,11},{8,4},{9,5},... | collective-permute-start | bytes 442376 | tf_op jit(solution)/shard_map/ppermute | solution.py:324
  6.8 0.0 collective-permute-start.1
  6.8 0.0 collective-permute-done.2.first_message
  6.8 0.0 collective-permute-done.3.second_message
  6.8 0.2 shard_map.43
  7.0 0.6 %collective-permute-start.4 = (f32[16,128]{1,0:T(8,128)S(1)}, f32[16,128]{1,0:T(8,128)S(1)}, u32[]{:S(2)}, u32[]{:S(2)}) collective-permute-start(f32[16,128]{1,0:T(8,128)S(1)} %get-tuple-element.29), channel_id=1, source_target_pairs={{0,4},{1,2},{2,1},{3,7},{4,0},{5,6},{6,5},{7,3},{8,12},{9,10},{10,... | collective-permute-start | bytes 24584 | tf_op jit(solution)/shard_map/ppermute | solution.py:324
  7.5 3.2 %collective-permute-start.5 = (f32[16,128]{1,0:T(8,128)S(1)}, f32[16,128]{1,0:T(8,128)S(1)}, u32[]{:S(2)}, u32[]{:S(2)}) collective-permute-start(f32[16,128]{1,0:T(8,128)S(1)} %get-tuple-element.30), channel_id=1, source_target_pairs={{0,1},{1,0},{2,3},{3,2},{4,5},{5,4},{6,7},{7,6},{8,9},{9,8},{10,11... | collective-permute-start | bytes 24584 | tf_op jit(solution)/shard_map/ppermute | solution.py:324
  10.7 0.0 collective-permute-done.first_message
  10.7 0.0 collective-permute-done.1.second_message
  10.7 2.1 %shard_map.42 = (bf16[8,96,512]{2,1,0:T(8,128)(2,1)S(1)}, f32[32,64]{1,0:T(8,128)S(1)}) custom-call(f32[8,32,512]{2,1,0:T(8,128)S(1)} %get-tuple-element.18.by_row, f32[8,8,512]{2,1,0:T(8,128)S(1)} %get-tuple-element.19.weights_by_row, f32[72,512]{1,0:T(8,128)S(1)} %collective-permute-done.first_message, f32[72,512]{1,0:T(8,128)S(1)} %collective-permute-done.1.second_message), custom_call_target="tpu_custom_call" | custom-call | tf_op jit(solution)/shard_map/pallas_call | solution.py:18
  12.8 0.0 collective-permute-done.4.first_message
  12.8 0.0 collective-permute-done.5.second_message
  12.8 0.8 %shard_map.44 = (f32[16,1,1152]{2,1,0:T(1,128)S(1)}, f32[32,256]{1,0:T(8,128)S(1)}) custom-call(f32[40,128]{1,0:T(8,128)S(1)} %get-tuple-element.27.left, f32[40,128]{1,0:T(8,128)S(1)} %get-tuple-element.28.right, f32[16,128]{1,0:T(8,128)S(1)} %collective-permute-done.4.first_message, f32[16,128]{1,0:T(8,128)S(1)} %collective-permute-done.5.second_message, ...), custom_call_target="tpu_custom_call" | custom-call | tf_op jit(solution)/shard_map/pallas_call | solution.py:18
  13.6 11.2 %all_to_all.5.parts = f32[16,1,1152]{2,1,0:T(1,128)S(1)} all-to-all(f32[16,1,1152]{2,1,0:T(1,128)S(1)} %get-tuple-element.33), channel_id=1, replica_groups=mesh['sec'=2,'row'=4,'col'=4] {'row','col'}, dimensions={0} | all-to-all | bytes 147456 | tf_op jit(solution)/shard_map/all_to_all | solution.py:360
  24.8 2.2 %shard_map.45 = (f32[32,8,512]{2,1,0:T(8,128)}, f32[32,32]{1,0:T(8,128)}) custom-call(bf16[8,96,512]{2,1,0:T(8,128)(2,1)S(1)} %get-tuple-element.22.second, f32[32,256]{1,0:T(8,128)S(1)} %get-tuple-element.32.edges, f32[16,1,1152]{2,1,0:T(1,128)S(1)} %all_to_all.5.parts), custom_call_target="tpu_custom_call" | custom-call | tf_op jit(solution)/shard_map/pallas_call | solution.py:18
Async XLA Ops:
  2.1 4.7 %collective-permute-start.2 = (f32[16,128]{1,0:T(8,128)S(1)}, f32[16,128]{1,0:T(8,128)S(1)}, u32[]{:S(2)}, u32[]{:S(2)}) collective-permute-start(f32[16,128]{1,0:T(8,128)S(1)} %get-tuple-element.25), channel_id=1, source_target_pairs={{0,16},{1,17},{2,18},{3,19},{4,8},{5,9},{6,10},{7,11},{8,4},{9,5},... | collective-permute-start | bytes 24584 | tf_op jit(solution)/shard_map/ppermute | solution.py:324
  5.2 1.6 %collective-permute-start.3 = (f32[16,128]{1,0:T(8,128)S(1)}, f32[16,128]{1,0:T(8,128)S(1)}, u32[]{:S(2)}, u32[]{:S(2)}) collective-permute-start(f32[16,128]{1,0:T(8,128)S(1)} %get-tuple-element.26), channel_id=1, source_target_pairs={{0,4},{1,5},{2,6},{3,7},{4,0},{5,1},{6,2},{7,3},{8,12},{9,13},{10,... | collective-permute-start | bytes 24584 | tf_op jit(solution)/shard_map/ppermute | solution.py:324
  5.2 5.4 %collective-permute-start = (f32[72,512]{1,0:T(8,128)S(1)}, f32[72,512]{1,0:T(8,128)S(1)}, u32[]{:S(2)}, u32[]{:S(2)}) collective-permute-start(f32[72,512]{1,0:T(8,128)S(1)} %get-tuple-element.20), channel_id=1, source_target_pairs={{0,16},{1,17},{2,18},{3,19},{4,8},{5,9},{6,10},{7,11},{8,4},{9,5},... | collective-permute-start | bytes 442376 | tf_op jit(solution)/shard_map/ppermute | solution.py:324
  6.8 3.9 %collective-permute-start.1 = (f32[72,512]{1,0:T(8,128)S(1)}, f32[72,512]{1,0:T(8,128)S(1)}, u32[]{:S(2)}, u32[]{:S(2)}) collective-permute-start(f32[72,512]{1,0:T(8,128)S(1)} %get-tuple-element.21), channel_id=1, source_target_pairs={{0,4},{1,5},{2,6},{3,7},{4,0},{5,1},{6,2},{7,3},{8,12},{9,13},{10,... | collective-permute-start | bytes 442376 | tf_op jit(solution)/shard_map/ppermute | solution.py:324
  7.0 5.8 %collective-permute-start.4 = (f32[16,128]{1,0:T(8,128)S(1)}, f32[16,128]{1,0:T(8,128)S(1)}, u32[]{:S(2)}, u32[]{:S(2)}) collective-permute-start(f32[16,128]{1,0:T(8,128)S(1)} %get-tuple-element.29), channel_id=1, source_target_pairs={{0,4},{1,2},{2,1},{3,7},{4,0},{5,6},{6,5},{7,3},{8,12},{9,10},{10,... | collective-permute-start | bytes 24584 | tf_op jit(solution)/shard_map/ppermute | solution.py:324
  7.5 5.3 %collective-permute-start.5 = (f32[16,128]{1,0:T(8,128)S(1)}, f32[16,128]{1,0:T(8,128)S(1)}, u32[]{:S(2)}, u32[]{:S(2)}) collective-permute-start(f32[16,128]{1,0:T(8,128)S(1)} %get-tuple-element.30), channel_id=1, source_target_pairs={{0,1},{1,0},{2,3},{3,2},{4,5},{5,4},{6,7},{7,6},{8,9},{9,8},{10,11... | collective-permute-start | bytes 24584 | tf_op jit(solution)/shard_map/ppermute | solution.py:324
